TPU v7x, 768 devices: a whole 4x8x12 slice. The times are simulated.
768 devices in a mesh: blk: 32 (over z_lo, x, core), narrow: 24 (over y, z_hi).
Axes of the slice: x: 4, y: 8, z: 12 (z_hi: 3, z_lo: 4; z = z_hi * 4 + z_lo), core: 2. Of those that a mesh axis runs over, the one named last changes fastest.
Arguments:
- image_features: bfloat16 [294912, 1152], P(('blk', 'narrow')), may hold values from -6 to 6
- head_weight: bfloat16 [1152, 1152], replicated, may hold values from -0.1875 to 0.1875
- text_embeddings: bfloat16 [294912, 1152], P(('blk', 'narrow')), may hold values from -0.1875 to 0.1875
- log_scale: float32 [1], replicated, may hold values from 1.5 to 2.5
- logit_bias: float32 [1], replicated, may hold values from -3 to -1
Outputs:
- text_grad: float32 [294912, 1152], P(('blk', 'narrow'))
- head_grad: float32 [1152, 1152], P('narrow', 'blk')
All inputs are finite; a program needn't handle non-finite values.
Results may differ from a plain program's by a relative error of at most 0.0051.
Values may be sent and summed in bfloat16 or wider, within the bound.
A program may use at most 128 MiB of HBM per device.

v0:
```python
import jax
import jax.numpy as jnp
from jax import lax
from jax.sharding import PartitionSpec as P

norm_eps = 1e-06


def passed_along(value, axis, steps):
    count = lax.axis_size(axis)
    pairs = [(source, (source + steps) % count) for source in range(count)]
    return lax.ppermute(value, axis, pairs)


def normalize(vector):
    inverse = lax.rsqrt(jnp.sum(vector * vector, axis=-1, keepdims=True) + norm_eps)
    return (vector * inverse, inverse)


def shards(image_features, head_weight, text_embeddings, log_scale, logit_bias):
    projected = jnp.dot(image_features, head_weight, preferred_element_type=jnp.float32)
    image_unit, image_inverse = normalize(projected)
    image_bf = image_unit.astype(jnp.bfloat16)
    text_unit, text_inverse = normalize(text_embeddings.astype(jnp.float32))
    text_bf = text_unit.astype(jnp.bfloat16)
    row_count = image_bf.shape[0]
    logit_scale = jnp.exp(log_scale[0])
    positives = 2.0 * jnp.eye(row_count, dtype=jnp.float32) - 1.0
    negatives = -jnp.ones((row_count, row_count), jnp.float32)

    def pair_grads(text_block, labels):
        scores = (
            logit_scale
            * jnp.einsum("id,jd->ij", image_bf, text_block, preferred_element_type=jnp.float32)
            + logit_bias[0]
        )
        coupling = (-labels * jax.nn.sigmoid(-labels * scores) * logit_scale).astype(jnp.bfloat16)
        image_part = jnp.dot(coupling, text_block, preferred_element_type=jnp.float32)
        text_part = jnp.einsum("ij,id->jd", coupling, image_bf, preferred_element_type=jnp.float32)
        return (image_part, text_part)

    image_first, text_first = pair_grads(text_bf, positives)
    text_prev, carried = (
        passed_along(text_bf.astype(jnp.float32), "blk", 1).astype(text_bf.dtype),
        passed_along(text_first, "blk", 1),
    )
    image_second, text_second = pair_grads(text_prev, negatives)
    text_total = passed_along(carried + text_second, "blk", -1)
    image_total = image_first + image_second
    text_grad = (
        text_total - text_unit * jnp.sum(text_unit * text_total, axis=-1, keepdims=True)
    ) * text_inverse
    image_delta = (
        (image_total - image_unit * jnp.sum(image_unit * image_total, axis=-1, keepdims=True))
        * image_inverse
    ).astype(jnp.bfloat16)
    head_rows = lax.psum_scatter(
        jnp.einsum("rf,rd->fd", image_features, image_delta, preferred_element_type=jnp.float32),
        "narrow",
        scatter_dimension=0,
        tiled=True,
    )
    head_share = lax.psum_scatter(head_rows, "blk", scatter_dimension=1, tiled=True)
    return (text_grad, head_share)


def solution(mesh):
    return jax.shard_map(
        shards,
        mesh=mesh,
        in_specs=(P(("blk", "narrow"), None), P(), P(("blk", "narrow"), None), P(), P()),
        out_specs=(P(("blk", "narrow"), None), P("narrow", "blk")),
        check_vma=False,
    )
```

profile of v0, /device:TPU:56, one launch (start us, length us, event | category | flops | bytes accessed | tf_op | source)
XLA Modules:
  0.0 719.0 jit_solution(11959316015661476051)
XLA Ops:
  7.2 0.0 copy-start
  7.2 0.0 copy-start.7
  7.2 0.0 reduce-scatter.6.cloned.1.call-start
  7.2 1.6 fusion.7
  8.8 1.4 fusion.30
  10.2 1.9 collective-permute-start.1
  12.2 1.5 multiply_reduce_fusion.1
  13.7 0.2 multiply_convert_fusion.1
  13.9 0.0 copy-start.2
  15.5 0.9 fusion.22
  16.4 0.7 fusion.28
  17.1 13.4 %collective-permute-done.1 = bf16[384,1152]{1,0:T(8,128)(2,1)S(1)} collective-permute-done((bf16[384,1152]{1,0:T(8,128)(2,1)S(1)}, bf16[384,1152]{1,0:T(8,128)(2,1)S(1)}, u32[]{:S(2)}, u32[]{:S(2)}) %collective-permute-start.1) | collective-permute-done | bytes 884768 | tf_op jit(solution)/shard_map/ppermute | solution.py:12
  30.5 0.7 fusion.23
  31.2 0.0 copy-start.8
  31.2 0.9 multiply_reduce_fusion
  32.1 0.4 copy-done.8
  32.5 4.3 convolution_bitcast_fusion
  36.8 6.9 copy.7
  43.6 0.0 reduce-scatter.6.cloned.1.call-update
  43.7 0.0 copy-start.3
  43.7 2.0 fusion.32
  45.7 1.9 collective-permute-start
  47.6 28.7 %collective-permute-done = f32[384,1152]{1,0:T(8,128)S(1)} collective-permute-done((f32[384,1152]{1,0:T(8,128)S(1)}, f32[384,1152]{1,0:T(8,128)S(1)}, u32[]{:S(2)}, u32[]{:S(2)}) %collective-permute-start) | collective-permute-done | bytes 1769504 | tf_op jit(solution)/shard_map/ppermute | solution.py:12
  76.4 1.9 convolution_add_fusion.1
  78.3 1.9 collective-permute-start.2
  80.2 1.3 dynamic-slice.4
  82.1 512.6 %reduce-scatter.6.cloned.1.call-done = f32[48,1152]{1,0:T(8,128)} async-done(((f32[1152,1152]{1,0:T(8,128)}), f32[48,1152]{1,0:T(8,128)}) %reduce-scatter.6.cloned.1.call-update) | async-done | bytes 221200
  594.8 2.0 copy.8
  596.7 79.0 %fusion = f32[48,48]{0,1:T(8,128)} fusion(f32[48,1152]{0,1:T(8,128)} %copy.8), kind=kCustom, calls=%all-reduce-scatter | all-reduce-scatter fusion | flops 73729 | bytes 234496
  675.8 0.8 slice
  676.6 1.3 collective-permute-start.3
  677.9 1.3 collective-permute-start.4
  679.2 1.3 collective-permute-start.10
  680.5 1.8 fusion.4
  682.3 1.3 collective-permute-start.5
  683.6 1.3 collective-permute-start.6
  684.9 0.0 copy-start.16
  684.9 1.3 collective-permute-start.7
  686.3 6.7 collective-permute-start.8
  693.0 0.6 copy-done.11
  693.6 6.5 collective-permute-start.9
  700.1 3.0 fusion.6
  703.2 0.6 copy-done.12
  703.8 0.0 copy-done.13
  703.8 0.0 copy-done.14
  703.8 0.6 copy-done.15
  704.4 7.1 concatenate
  711.5 0.6 constant_dynamic-slice_fusion
  (33 shorter events, 0.1 us)
Async XLA Ops:
  7.2 5.0 copy-start
  7.2 5.0 copy-start.7
  7.2 587.6 %reduce-scatter.6.cloned.1.call-start = ((), (), s32[]{:S(2)}) async-start(), calls=%async_computation.1 | async-start | bytes 5529600
  10.2 20.3 %collective-permute-start.1 = (bf16[384,1152]{1,0:T(8,128)(2,1)S(1)}, bf16[384,1152]{1,0:T(8,128)(2,1)S(1)}, u32[]{:S(2)}, u32[]{:S(2)}) collective-permute-start(bf16[384,1152]{1,0:T(8,128)(2,1)S(1)} %fusion.30), channel_id=1, source_target_pairs={{0,24},{24,48},{48,72},{72,96},{96,120},{120,144},{144,168},{168,1... | collective-permute-start | bytes 2654216 | tf_op jit(solution)/shard_map/ppermute | solution.py:12
  13.7 1.8 copy-start.1
  13.9 16.6 %copy-start.2 = (bf16[384,1152]{1,0:T(8,128)(2,1)}, bf16[384,1152]{1,0:T(8,128)(2,1)S(1)}, u32[]{:S(2)}) copy-start(bf16[384,1152]{1,0:T(8,128)(2,1)S(1)} %multiply_convert_fusion.1) | copy-start | bytes 2654212
  16.4 14.1 %copy-start.6 = (bf16[384,384]{1,0:T(8,128)(2,1)}, bf16[384,384]{1,0:T(8,128)(2,1)S(1)}, u32[]{:S(2)}) copy-start(bf16[384,384]{1,0:T(8,128)(2,1)S(1)} %fusion.22) | copy-start | bytes 884740
  31.2 0.9 copy-start.4
  31.2 1.3 copy-start.8
  43.7 32.7 %copy-start.3 = (bf16[384,1152]{1,0:T(8,128)(2,1)S(1)}, bf16[384,1152]{1,0:T(8,128)(2,1)}, u32[]{:S(2)}) copy-start(bf16[384,1152]{1,0:T(8,128)(2,1)} %copy-done.2) | copy-start | bytes 2654212
  43.7 32.7 %copy-start.5 = (bf16[384,384]{1,0:T(8,128)(2,1)S(1)}, bf16[384,384]{1,0:T(8,128)(2,1)}, u32[]{:S(2)}) copy-start(bf16[384,384]{1,0:T(8,128)(2,1)} %copy-done.4) | copy-start | bytes 884740
  45.7 30.7 %collective-permute-start = (f32[384,1152]{1,0:T(8,128)S(1)}, f32[384,1152]{1,0:T(8,128)S(1)}, u32[]{:S(2)}, u32[]{:S(2)}) collective-permute-start(f32[384,1152]{1,0:T(8,128)S(1)} %fusion.32), channel_id=1, source_target_pairs={{0,24},{24,48},{48,72},{72,96},{96,120},{120,144},{144,168},{168,1... | collective-permute-start | bytes 5308424 | tf_op jit(solution)/shard_map/ppermute | solution.py:12
  78.3 602.2 %collective-permute-start.2 = (f32[384,1152]{1,0:T(8,128)}, f32[384,1152]{1,0:T(8,128)}, u32[]{:S(2)}, u32[]{:S(2)}) collective-permute-start(f32[384,1152]{1,0:T(8,128)} %convolution_add_fusion.1), channel_id=1, source_target_pairs={{0,744},{24,0},{48,24},{72,48},{96,72},{120,96},{144,120},{168,144... | collective-permute-start | bytes 5308424 | tf_op jit(solution)/shard_map/ppermute | solution.py:12
  675.8 6.5 copy-start.9
  676.6 9.7 %collective-permute-start.3 = (f32[48,48]{0,1:T(8,128)}, f32[48,48]{0,1:T(8,128)S(1)}, u32[]{:S(2)}, u32[]{:S(2)}) collective-permute-start(f32[48,48]{0,1:T(8,128)} %fusion), channel_id=1, source_target_pairs={{0,24},{24,48},{48,72},{72,96},{96,120},{120,144},{144,168},{168,1... | collective-permute-start | bytes 27656
  677.9 15.1 %collective-permute-start.4 = (f32[48,48]{0,1:T(8,128)}, f32[48,48]{0,1:T(8,128)S(1)}, u32[]{:S(2)}, u32[]{:S(2)}) collective-permute-start(f32[48,48]{0,1:T(8,128)} %fusion), channel_id=1, source_target_pairs={{0,48},{24,72},{48,96},{72,120},{96,144},{120,168},{144,192},{168,... | collective-permute-start | bytes 27656
  679.2 5.8 collective-permute-start.10
  682.3 20.9 %collective-permute-start.5 = (f32[48,48]{0,1:T(8,128)S(1)}, f32[48,48]{0,1:T(8,128)S(1)}, u32[]{:S(2)}, u32[]{:S(2)}) collective-permute-start(f32[48,48]{0,1:T(8,128)S(1)} %copy-done.9), channel_id=1, source_target_pairs={{0,72},{24,96},{48,120},{72,144},{96,168},{120,192},{144,216},{168... | collective-permute-start | bytes 27656
  683.6 19.6 %collective-permute-start.6 = (f32[48,48]{0,1:T(8,128)S(1)}, f32[48,48]{0,1:T(8,128)S(1)}, u32[]{:S(2)}, u32[]{:S(2)}) collective-permute-start(f32[48,48]{0,1:T(8,128)S(1)} %copy-done.9), channel_id=1, source_target_pairs={{0,96},{24,120},{48,144},{72,168},{96,192},{120,216},{144,240},{16... | collective-permute-start | bytes 27656
  684.9 8.1 %copy-start.16 = (f32[48,36]{0,1:T(8,128)}, f32[48,36]{0,1:T(8,128)S(1)}, u32[]{:S(2)}) copy-start(f32[48,36]{0,1:T(8,128)S(1)} %collective-permute-done.10) | copy-start | bytes 20740
  684.9 18.3 %collective-permute-start.7 = (f32[48,48]{0,1:T(8,128)S(1)}, f32[48,48]{0,1:T(8,128)S(1)}, u32[]{:S(2)}, u32[]{:S(2)}) collective-permute-start(f32[48,48]{0,1:T(8,128)S(1)} %copy-done.9), channel_id=1, source_target_pairs={{0,120},{24,144},{48,168},{72,192},{96,216},{120,240},{144,264},{1... | collective-permute-start | bytes 27656
  686.3 6.7 copy-start.10
  686.3 17.0 %collective-permute-start.8 = (f32[48,48]{0,1:T(8,128)S(1)}, f32[48,48]{0,1:T(8,128)S(1)}, u32[]{:S(2)}, u32[]{:S(2)}) collective-permute-start(f32[48,48]{0,1:T(8,128)S(1)} %copy-done.9), channel_id=1, source_target_pairs={{0,144},{24,168},{48,192},{72,216},{96,240},{120,264},{144,288},{1... | collective-permute-start | bytes 27656
  693.0 0.6 copy-start.11
  693.6 10.8 %collective-permute-start.9 = (f32[48,48]{0,1:T(8,128)S(1)}, f32[48,48]{0,1:T(8,128)}, u32[]{:S(2)}, u32[]{:S(2)}) collective-permute-start(f32[48,48]{0,1:T(8,128)S(1)} %copy-done.9), channel_id=1, source_target_pairs={{0,168},{24,192},{48,216},{72,240},{96,264},{120,288},{144,312},{1... | collective-permute-start | bytes 27656
  703.2 0.6 copy-start.12
  703.2 0.6 copy-start.13
  703.2 0.6 copy-start.14
  703.8 0.6 copy-start.15
Sparse Core Ops, SparseCore 0:
  43.8 550.9 reduce-scatter.5
where the time goes:
time: 723 us; the launch traced here: 719 us
  waiting for transfers between devices  555 us (77%)
  blocking collectives  79 us (11%)
  starting transfers between devices  26.8 us (4%)
  local copies, waits for them, and re-layouts  20.9 us (3%)
  between operations  16.6 us (2%)
  matrix products  12.9 us (2%)
  other arithmetic  8.01 us (1%)
    unnamed x10, waiting for transfers between devices  513 us
    unnamed x1, blocking collectives  79 us
    ppermute x3, waiting for transfers between devices, passed_along(): return lax.ppermute(value, axis, pairs)  42.1 us
    unnamed x9, starting transfers between devices  21 us
    unnamed x40, local copies, waits for them, and re-layouts  20.9 us
  transfers between devices with their start and end apart: 12, of which 3 were waited for; matrix products, arithmetic and copies ran while one was open for 13% of the time, Pallas kernels for 0%

commit v1 on v0

v1 whole, which is shorter than its diff:
```python
import jax
import jax.numpy as jnp
from jax import lax
from jax.experimental import pallas as pl
from jax.experimental.pallas import tpu as pltpu
from jax.sharding import PartitionSpec as P

MESH = pl.DeviceIdType.MESH
F32 = jnp.float32
BF = jnp.bfloat16
EPS = 1e-06
NX, NY, ZL, ZH = 4, 8, 4, 3
R = 384
D = 1152
CH = 384
NCH = D // CH
G = 36
PIECE = 128


def mm(a, b, dims):
    return lax.dot_general(a, b, (dims, ((), ())), preferred_element_type=F32)


NN = ((1,), (0,))
NT = ((1,), (1,))
TN = ((0,), (0,))


def kernel(
    x_hbm, w_hbm, t_hbm, ls_ref, lb_ref,
    tg_ref, hg_ref,
    xb, wb, traw, tb, proj, ib, cb, c1b, c2b, dyo, dys, dyr, dtf, pf, dtb, hacc,
    xs, xr, sc, zs, zf, zr, yf, ys, yr, hs, hr,
    lsem, x2s, x2r, fws, fwr, dts, dtr, pxs, pxr, pts, ptr, dyss, dyrs,
    xss, xrs, zss, zrs, yss, yrs, hss, hrs,
):
    blk = lax.axis_index("blk")
    nar = lax.axis_index("narrow")
    c = blk % 2
    x = (blk // 2) % NX
    zl = blk // (2 * NX)
    y = nar // ZH
    zh = nar % ZH

    def dev(x_, zl_, c_, y_, zh_):
        return ((zl_ * NX + x_) * 2 + c_, y_ * ZH + zh_)

    partner = dev(x, zl, 1 - c, y, zh)
    chip = blk // 2
    chips = NX * ZL
    prev = (chip + chips - 1) % chips
    nxt = (chip + 1) % chips

    bar = pltpu.get_barrier_semaphore()

    def hello(d):
        pl.semaphore_signal(bar, inc=1, device_id=d, device_id_type=MESH)

    lx = pltpu.make_async_copy(x_hbm, xb.at[pl.ds(pl.multiple_of(c * R, R), R)], lsem.at[0])
    lw = pltpu.make_async_copy(w_hbm, wb, lsem.at[1])
    lt = pltpu.make_async_copy(t_hbm, traw, lsem.at[2])
    lt.start()
    lx.start()
    lw.start()

    hello(partner)
    hello((nxt * 2, nar))
    for d in range(1, NX):
        hello(dev((x + d) % NX, zl, c, y, zh))
    for d in range(1, ZL):
        hello(dev(x, (zl + d) % ZL, c, y, zh))
    for d in range(1, NY):
        hello(dev(x, zl, c, (y + d) % NY, zh))
    for d in range(1, ZH):
        hello(dev(x, zl, c, y, (zh + d) % ZH))

    base = 1 + (NX - 1) + (ZL - 1) + (NY - 1) + (ZH - 1)

    @pl.when(c == 0)
    def _():
        pl.semaphore_wait(bar, base + 2)

    @pl.when(c == 1)
    def _():
        pl.semaphore_wait(bar, base)

    def rcopy(src, dst, ss, rs, device):
        return pltpu.make_async_remote_copy(
            src_ref=src, dst_ref=dst, send_sem=ss, recv_sem=rs, device_id=device, device_id_type=MESH
        )

    def x2copy(piece, core, slot):
        return rcopy(
            x_hbm.at[pl.ds(piece * PIECE, PIECE)],
            xb.at[pl.ds(2 * R + piece * PIECE, PIECE)],
            x2s.at[piece],
            x2r.at[slot],
            (prev * 2 + core, nar),
        )

    @pl.when(c == 0)
    def _():
        x2copy(0, 0, 0).start()
        x2copy(2, 1, 0).start()
        x2copy(1, 0, 1).start()

    own = pl.ds(pl.multiple_of(c * R, R), R)
    other = pl.ds(pl.multiple_of((1 - c) * R, R), R)
    px = rcopy(x_hbm, xb.at[own], pxs, pxr, partner)
    px.start()

    lt.wait()

    def text_unit():
        t = traw[...].astype(F32)
        inv = lax.rsqrt(jnp.sum(t * t, axis=-1, keepdims=True) + EPS)
        return t * inv, inv

    tb[own, :] = text_unit()[0].astype(BF)
    pt = rcopy(tb.at[own], tb.at[own], pts, ptr, partner)
    pt.start()

    scale = jnp.exp(jnp.full((1, R), ls_ref[0], F32))
    bias = lb_ref[0]

    def coupling(img, text, positive):
        s = scale * mm(img, text, NT) + bias
        if not positive:
            return (jax.nn.sigmoid(s) * scale).astype(BF)
        rows, cols = s.shape
        diag = lax.broadcasted_iota(jnp.int32, (rows, cols), 0) == lax.broadcasted_iota(
            jnp.int32, (rows, cols), 1
        )
        g = jax.nn.sigmoid(jnp.where(diag, -s, s))
        return (jnp.where(diag, -g, g) * scale).astype(BF)

    def project(rows, slot, n):
        a = xb[rows, :]
        total = jnp.zeros((n, 1), F32)
        for k in range(NCH):
            p = mm(a, wb[:, k * CH : (k + 1) * CH], NN)
            proj[slot, k * CH : (k + 1) * CH] = p
            total = total + jnp.sum(p * p, axis=-1, keepdims=True)
        inv = lax.rsqrt(total + EPS)
        ib[slot, :] = (proj[slot, :] * inv).astype(BF)
        return inv

    def delta_out(tot, slot, inv, col, n):
        unit = proj[slot, :] * inv
        dl = (tot - unit * jnp.sum(unit * tot, axis=-1, keepdims=True)) * inv
        dtf[:, 0:n] = dl.astype(BF).astype(F32).T
        for q in range(2):
            for xx in range(NX):
                for z in range(ZL):
                    o = ((z * NX + xx) * 2 + q) * G
                    pf[z * G : (z + 1) * G, 0:n] = dtf[o : o + G, 0:n]
                dtb[q, xx * ZL * G : (xx + 1) * ZL * G, col] = pf[:, 0:n].astype(BF)

    def dtcopy(col, i):
        return rcopy(
            dtb.at[1 - c, :, col], dtb.at[1 - c, :, col], dts.at[i], dtr.at[i], partner
        )

    lx.wait()
    lw.wait()
    first = pl.ds(0, R)
    inv0 = project(own, first, R)
    cb[...] = coupling(ib[first, :], tb[own, :], True)
    dyo[...] = mm(cb[...], tb[own, :], NN)
    pt.wait()

    @pl.when(c == 1)
    def _():
        c1b[...] = coupling(ib[first, :], tb[0:R, :], False)
        dyo[...] += mm(c1b[...], tb[0:R, :], NN)

    owncol = pl.ds(pl.multiple_of(c * R, R), R)
    delta_out(dyo[...], first, inv0, owncol, R)
    dt0 = dtcopy(owncol, 0)
    dt0.start()

    dyo[...] = mm(cb[...], ib[first, :], TN)

    @pl.when(c == 1)
    def _():
        dys[...] = mm(c1b[...], ib[first, :], TN).astype(BF)

    px.wait()
    dt0.wait()
    for k in range(NCH):
        ks = slice(k * CH, (k + 1) * CH)
        hacc[:, ks] = mm(dtb[c, :, 0 : 2 * R], xb[0 : 2 * R, ks], NN)

    def fwcopy(g, slot):
        rows = pl.ds(pl.multiple_of(2 * R + g * PIECE, PIECE), PIECE)
        return rcopy(xb.at[rows], xb.at[rows], fws.at[slot], fwr.at[slot], partner)

    def colof(g):
        return pl.ds(pl.multiple_of(2 * R + g * PIECE, PIECE), PIECE)

    def piece(g, slot):
        rcopy(
            x_hbm.at[pl.ds(0, PIECE)], xb.at[colof(g)], x2s.at[0], x2r.at[slot], partner
        ).wait_recv()
        fwcopy(g, slot).start()
        at = pl.ds(R + slot * PIECE, PIECE)
        inv = project(colof(g), at, PIECE)
        cp = coupling(ib[at, :], tb[R : 2 * R, :], False)
        c2b[slot * PIECE : (slot + 1) * PIECE, :] = cp
        delta_out(mm(cp, tb[R : 2 * R, :], NN), at, inv, colof(g), PIECE)
        dtcopy(colof(g), 1 + slot).start()

    piece(2 * c, 0)

    @pl.when(c == 0)
    def _():
        piece(1, 1)

    @pl.when(c == 0)
    def _():
        fwcopy(0, 0).wait_send()
        fwcopy(1, 1).wait_send()
        dtcopy(colof(0), 1).wait_send()
        dtcopy(colof(1), 2).wait_send()
        fwcopy(2, 0).wait_recv()
        dtcopy(colof(2), 1).wait_recv()

    @pl.when(c == 1)
    def _():
        fwcopy(2, 0).wait_send()
        dtcopy(colof(2), 1).wait_send()
        fwcopy(0, 0).wait_recv()
        fwcopy(1, 1).wait_recv()
        dtcopy(colof(0), 1).wait_recv()
        dtcopy(colof(1), 2).wait_recv()

    def xcopy(k, d):
        i = k * (NX - 1) + d - 1
        to = (x + d) % NX
        return rcopy(
            xs.at[k, to], xr.at[k, d - 1], xss.at[i], xrs.at[i], dev(to, zl, c, y, zh)
        )

    for k in range(NCH):
        ks = slice(k * CH, (k + 1) * CH)
        h = hacc[:, ks] + mm(dtb[c, :, 2 * R : 3 * R], xb[2 * R : 3 * R, ks], NN)
        hacc[:, ks] = h
        for xx in range(NX):
            xs[k, xx] = h[xx * ZL * G : (xx + 1) * ZL * G, :].astype(BF)
        for d in range(1, NX):
            xcopy(k, d).start()

    dyc = rcopy(dys, dyr, dyss, dyrs, partner)

    @pl.when(c == 0)
    def _():
        dys[...] = mm(c2b[...], ib[pl.ds(R, 2 * PIECE), :], TN).astype(BF)

    dyc.start()

    @pl.when(c == 1)
    def _():
        dyo[...] += mm(c2b[0:PIECE, :], ib[pl.ds(R, PIECE), :], TN)

    dyc.wait()
    tu, tinv = text_unit()
    tt = dyo[...] + dyr[...].astype(F32)
    tg_ref[...] = (tt - tu * jnp.sum(tu * tt, axis=-1, keepdims=True)) * tinv

    def zcopy(k, d):
        i = k * (ZL - 1) + d - 1
        to = (zl + d) % ZL
        return rcopy(
            zs.at[k, to], zr.at[k, d - 1], zss.at[i], zrs.at[i], dev(x, to, c, y, zh)
        )

    sc[ZL * G :, :] = jnp.zeros((16, CH), F32)
    rows = pl.ds(pl.multiple_of(x * ZL * G, ZL * G), ZL * G)
    for k in range(NCH):
        s = hacc[rows, k * CH : (k + 1) * CH]
        for d in range(1, NX):
            xcopy(k, d).wait_recv()
            s = s + xr[k, d - 1].astype(F32)
        sc[0 : ZL * G, :] = s
        for z in range(ZL):
            p = sc[z * G : z * G + 48, :]
            zf[k, z] = p
            zs[k, z] = p.astype(BF)
        for d in range(1, ZL):
            zcopy(k, d).start()

    for k in range(NCH):
        s = zf[k, zl]
        for d in range(1, ZL):
            zcopy(k, d).wait_recv()
            s = s + zr[k, d - 1].astype(F32)
        yf[:, k * CH : (k + 1) * CH] = s
        ys[:, k * CH : (k + 1) * CH] = s.astype(BF)

    def window(i):
        return pl.ds(pl.multiple_of(i * 128, 128), 256)

    def ycopy(d):
        to = (y + d) % NY
        return rcopy(
            ys.at[:, window(to)], yr.at[d - 1], yss.at[d - 1], yrs.at[d - 1], dev(x, zl, c, to, zh)
        )

    for d in range(1, NY):
        ycopy(d).start()
    s = yf[:, window(y)]
    for d in range(1, NY):
        ycopy(d).wait_recv()
        s = s + yr[d - 1].astype(F32)

    hs[...] = s.astype(BF)

    def hcopy(d):
        return rcopy(hs, hr.at[d - 1], hss.at[d - 1], hrs.at[d - 1], dev(x, zl, c, y, (zh + d) % ZH))

    for d in range(1, ZH):
        hcopy(d).start()
    for d in range(1, ZH):
        hcopy(d).wait_recv()
        s = s + hr[d - 1].astype(F32)
    s = pltpu.roll(s, (256 - (16 * y + 48 * zh)) % 256, 1)
    hg_ref[...] = s[:, 0:128].T[0:48, 0:G]

    @pl.when(c == 0)
    def _():
        for p, core, slot in ((0, 0, 0), (2, 1, 0), (1, 0, 1)):
            x2copy(p, core, slot).wait_send()

    for k in range(NCH):
        for d in range(1, NX):
            xcopy(k, d).wait_send()
        for d in range(1, ZL):
            zcopy(k, d).wait_send()
    for d in range(1, NY):
        ycopy(d).wait_send()
    for d in range(1, ZH):
        hcopy(d).wait_send()


def shards(image_features, head_weight, text_embeddings, log_scale, logit_bias):
    anyspec = pl.BlockSpec(memory_space=pl.ANY)
    smem = pl.BlockSpec(memory_space=pltpu.SMEM)
    vmem = pl.BlockSpec(memory_space=pltpu.VMEM)
    dma = pltpu.SemaphoreType.DMA
    V = pltpu.VMEM
    return pl.pallas_call(
        kernel,
        out_shape=(jax.ShapeDtypeStruct((R, D), F32), jax.ShapeDtypeStruct((48, G), F32)),
        in_specs=[anyspec, anyspec, anyspec, smem, smem],
        out_specs=(vmem, vmem),
        scratch_shapes=[
            V((3 * R, D), BF),
            V((D, D), BF),
            V((R, D), BF),
            V((2 * R, D), BF),
            V((R + 2 * PIECE, D), F32),
            V((R + 2 * PIECE, D), BF),
            V((R, R), BF),
            V((R, R), BF),
            V((2 * PIECE, R), BF),
            V((R, D), F32),
            V((R, D), BF),
            V((R, D), BF),
            V((D, R), F32),
            V((ZL * G, R), F32),
            V((2, D // 2, D), BF),
            V((D // 2, D), F32),
            V((NCH, NX, ZL * G, CH), BF),
            V((NCH, NX - 1, ZL * G, CH), BF),
            V((ZL * G + 16, CH), F32),
            V((NCH, ZL, 48, CH), BF),
            V((NCH, ZL, 48, CH), F32),
            V((NCH, ZL - 1, 48, CH), BF),
            V((48, D), F32),
            V((48, D), BF),
            V((NY - 1, 48, 256), BF),
            V((48, 256), BF),
            V((ZH - 1, 48, 256), BF),
            dma((3,)), dma((3,)), dma((2,)), dma((2,)), dma((2,)), dma((3,)), dma((3,)),
            dma, dma, dma, dma, dma, dma,
            dma((NCH * (NX - 1),)), dma((NCH * (NX - 1),)),
            dma((NCH * (ZL - 1),)), dma((NCH * (ZL - 1),)),
            dma((NY - 1,)), dma((NY - 1,)), dma((ZH - 1,)), dma((ZH - 1,)),
        ],
        compiler_params=pltpu.CompilerParams(
            collective_id=0, has_side_effects=True, vmem_limit_bytes=56 * 2**20
        ),
        name="siglip_backward",
    )(image_features, head_weight, text_embeddings, log_scale, logit_bias)


def solution(mesh):
    return jax.shard_map(
        shards,
        mesh=mesh,
        in_specs=(P(("blk", "narrow"), None), P(), P(("blk", "narrow"), None), P(), P()),
        out_specs=(P(("blk", "narrow"), None), P("narrow", "blk")),
        check_vma=False,
    )
```

time: 723 us -> 76.1 us (0.11)
  the two profiles are of different devices: /device:TPU:56 before, /device:TPU:64 now
where the time goes in v1:
time: 76.1 us; the launch traced here: 75.9 us
  Pallas kernels  69.7 us (92%)
  local copies, waits for them, and re-layouts  4.22 us (6%)
  between operations  1.93 us (3%)
    pallas_call x1, Pallas kernels, shards(): pl.pallas_call(kernel, out_shape=(jax.ShapeDtypeStruct((R, D), F32), jax....  69.7 us
    unnamed x1, local copies, waits for them, and re-layouts  2.8 us

profile of v1, /device:TPU:64, one launch (start us, length us, event | category | flops | bytes accessed | tf_op | source)
XLA Modules:
  0.0 75.9 jit_solution(17637643451052462718)
XLA Ops:
  1.9 69.7 %siglip_backward.1 = (f32[384,1152]{1,0:T(8,128)}, f32[48,36]{1,0:T(8,128)}) custom-call(bf16[384,1152]{1,0:T(8,128)(2,1)} %x_hbm.1, bf16[1152,1152]{1,0:T(8,128)(2,1)} %w_hbm.1, bf16[384,1152]{1,0:T(8,128)(2,1)} %t_hbm.1, f32[1]{0:T(128)S(6)} %copy.9.ls_ref, f32[1]{0:T(128)S(6)} %copy.10.lb_ref), custom_call_target="tpu_custom_call" | custom-call | tf_op jit(solution)/shard_map/siglip_backward/pallas_call | solution.py:352
  71.7 1.4 %copy.7 = f32[48,36]{0,1:T(8,128)} copy(f32[48,36]{1,0:T(8,128)} %get-tuple-element.3) | data formatting | bytes 13824 | tf_op jit(solution)/shard_map/siglip_backward/pallas_call | solution.py:352
  73.1 2.8 %copy.11 = f32[384,1152]{1,0:T(8,128)} copy(f32[384,1152]{1,0:T(8,128)} %get-tuple-element.6) | data formatting | bytes 3538944

commit v2 on v1

--- a/solution.py
+++ b/solution.py
@@ -16,6 +16,8 @@
 NCH = D // CH
 G = 36
 PIECE = 128
+CHUNKS = ((0, 512), (512, 384), (896, 256))
+WINDOWS = ((0, 1, 2), (3, 4, 5), (6, 7))
 
 
 def mm(a, b, dims):
@@ -31,10 +33,11 @@
     x_hbm, w_hbm, t_hbm, ls_ref, lb_ref,
     tg_ref, hg_ref,
     xb, wb, traw, tb, proj, ib, cb, c1b, c2b, dyo, dys, dyr, dtf, pf, dtb, hacc,
-    xs, xr, sc, zs, zf, zr, yf, ys, yr, hs, hr,
+    xs0, xs1, xs2, xr0, xr1, xr2, sc, zs0, zs1, zs2, zf, zr0, zr1, zr2, yf, ys, yr, hs, hf, hr,
     lsem, x2s, x2r, fws, fwr, dts, dtr, pxs, pxr, pts, ptr, dyss, dyrs,
     xss, xrs, zss, zrs, yss, yrs, hss, hrs,
 ):
+    xs, xr, zs, zr = (xs0, xs1, xs2), (xr0, xr1, xr2), (zs0, zs1, zs2), (zr0, zr1, zr2)
     blk = lax.axis_index("blk")
     nar = lax.axis_index("narrow")
     c = blk % 2
@@ -239,16 +242,16 @@
         i = k * (NX - 1) + d - 1
         to = (x + d) % NX
         return rcopy(
-            xs.at[k, to], xr.at[k, d - 1], xss.at[i], xrs.at[i], dev(to, zl, c, y, zh)
-        )
-
-    for k in range(NCH):
-        ks = slice(k * CH, (k + 1) * CH)
+            xs[k].at[to], xr[k].at[d - 1], xss.at[i], xrs.at[i], dev(to, zl, c, y, zh)
+        )
+
+    for k, (o, w) in enumerate(CHUNKS):
+        ks = slice(o, o + w)
         h = hacc[:, ks] + mm(dtb[c, :, 2 * R : 3 * R], xb[2 * R : 3 * R, ks], NN)
         hacc[:, ks] = h
         for xx in range(NX):
-            xs[k, xx] = h[xx * ZL * G : (xx + 1) * ZL * G, :].astype(BF)
-        for d in range(1, NX):
+            xs[k][xx] = h[xx * ZL * G : (xx + 1) * ZL * G, :].astype(BF)
+        for d in (2, 1, 3):
             xcopy(k, d).start()
 
     dyc = rcopy(dys, dyr, dyss, dyrs, partner)
@@ -272,60 +275,74 @@
         i = k * (ZL - 1) + d - 1
         to = (zl + d) % ZL
         return rcopy(
-            zs.at[k, to], zr.at[k, d - 1], zss.at[i], zrs.at[i], dev(x, to, c, y, zh)
-        )
-
-    sc[ZL * G :, :] = jnp.zeros((16, CH), F32)
+            zs[k].at[to], zr[k].at[d - 1], zss.at[i], zrs.at[i], dev(x, to, c, y, zh)
+        )
+
+    def ycopy(to):
+        slot = (y - to + NY) % NY - 1
+        return rcopy(
+            ys.at[:, to * 128 : to * 128 + 256],
+            yr.at[slot],
+            yss.at[to],
+            yrs.at[slot],
+            dev(x, zl, c, to, zh),
+        )
+
+    sc[ZL * G :, :] = jnp.zeros((16, sc.shape[1]), F32)
     rows = pl.ds(pl.multiple_of(x * ZL * G, ZL * G), ZL * G)
-    for k in range(NCH):
-        s = hacc[rows, k * CH : (k + 1) * CH]
+
+    def after_x(k):
+        o, w = CHUNKS[k]
+        s = hacc[rows, o : o + w]
         for d in range(1, NX):
             xcopy(k, d).wait_recv()
-            s = s + xr[k, d - 1].astype(F32)
-        sc[0 : ZL * G, :] = s
+            s = s + xr[k][d - 1].astype(F32)
+        sc[0 : ZL * G, 0:w] = s
         for z in range(ZL):
-            p = sc[z * G : z * G + 48, :]
-            zf[k, z] = p
-            zs[k, z] = p.astype(BF)
+            p = sc[z * G : z * G + 48, 0:w]
+            zf[z, :, o : o + w] = p
+            zs[k][z] = p.astype(BF)
         for d in range(1, ZL):
             zcopy(k, d).start()
 
-    for k in range(NCH):
-        s = zf[k, zl]
+    def after_z(k):
+        o, w = CHUNKS[k]
+        s = zf[zl, :, o : o + w]
         for d in range(1, ZL):
             zcopy(k, d).wait_recv()
-            s = s + zr[k, d - 1].astype(F32)
-        yf[:, k * CH : (k + 1) * CH] = s
-        ys[:, k * CH : (k + 1) * CH] = s.astype(BF)
-
-    def window(i):
-        return pl.ds(pl.multiple_of(i * 128, 128), 256)
-
-    def ycopy(d):
-        to = (y + d) % NY
-        return rcopy(
-            ys.at[:, window(to)], yr.at[d - 1], yss.at[d - 1], yrs.at[d - 1], dev(x, zl, c, to, zh)
-        )
-
+            s = s + zr[k][d - 1].astype(F32)
+        yf[:, o : o + w] = s
+        ys[:, o : o + w] = s.astype(BF)
+        for to in WINDOWS[k]:
+            pl.when(y != to)(ycopy(to).start)
+
+    after_x(0)
+    after_x(1)
+    after_z(0)
+    after_x(2)
+    after_z(1)
+    after_z(2)
+    s = yf[:, pl.ds(pl.multiple_of(y * 128, 128), 256)]
     for d in range(1, NY):
-        ycopy(d).start()
-    s = yf[:, window(y)]
-    for d in range(1, NY):
-        ycopy(d).wait_recv()
+        rcopy(ys.at[:, 0:256], yr.at[d - 1], yss.at[0], yrs.at[d - 1], partner).wait_recv()
         s = s + yr[d - 1].astype(F32)
 
-    hs[...] = s.astype(BF)
+    for z in range(ZH):
+        p = pltpu.roll(s, (256 - (16 * y + 48 * z)) % 256, 1)[:, 0:128]
+        hf[z] = p
+        hs[z] = p.astype(BF)
 
     def hcopy(d):
-        return rcopy(hs, hr.at[d - 1], hss.at[d - 1], hrs.at[d - 1], dev(x, zl, c, y, (zh + d) % ZH))
+        to = (zh + d) % ZH
+        return rcopy(hs.at[to], hr.at[d - 1], hss.at[d - 1], hrs.at[d - 1], dev(x, zl, c, y, to))
 
     for d in range(1, ZH):
         hcopy(d).start()
+    s = hf[zh]
     for d in range(1, ZH):
         hcopy(d).wait_recv()
         s = s + hr[d - 1].astype(F32)
-    s = pltpu.roll(s, (256 - (16 * y + 48 * zh)) % 256, 1)
-    hg_ref[...] = s[:, 0:128].T[0:48, 0:G]
+    hg_ref[...] = s[0:G, 0:48]
 
     @pl.when(c == 0)
     def _():
@@ -337,22 +354,22 @@
             xcopy(k, d).wait_send()
         for d in range(1, ZL):
             zcopy(k, d).wait_send()
-    for d in range(1, NY):
-        ycopy(d).wait_send()
+    for to in range(NY):
+        pl.when(y != to)(ycopy(to).wait_send)
     for d in range(1, ZH):
         hcopy(d).wait_send()
 
 
 def shards(image_features, head_weight, text_embeddings, log_scale, logit_bias):
-    anyspec = pl.BlockSpec(memory_space=pl.ANY)
+    hbm = pl.BlockSpec(memory_space=pltpu.HBM)
+    vmem = pl.BlockSpec(memory_space=pltpu.VMEM)
     smem = pl.BlockSpec(memory_space=pltpu.SMEM)
-    vmem = pl.BlockSpec(memory_space=pltpu.VMEM)
     dma = pltpu.SemaphoreType.DMA
     V = pltpu.VMEM
-    return pl.pallas_call(
+    text_grad, head_t = pl.pallas_call(
         kernel,
-        out_shape=(jax.ShapeDtypeStruct((R, D), F32), jax.ShapeDtypeStruct((48, G), F32)),
-        in_specs=[anyspec, anyspec, anyspec, smem, smem],
+        out_shape=(pltpu.VMEM((R, D), F32), pltpu.VMEM((G, 48), F32)),
+        in_specs=[hbm, hbm, hbm, smem, smem],
         out_specs=(vmem, vmem),
         scratch_shapes=[
             V((3 * R, D), BF),
@@ -371,28 +388,37 @@
             V((ZL * G, R), F32),
             V((2, D // 2, D), BF),
             V((D // 2, D), F32),
-            V((NCH, NX, ZL * G, CH), BF),
-            V((NCH, NX - 1, ZL * G, CH), BF),
-            V((ZL * G + 16, CH), F32),
-            V((NCH, ZL, 48, CH), BF),
-            V((NCH, ZL, 48, CH), F32),
-            V((NCH, ZL - 1, 48, CH), BF),
+            *[V((NX, ZL * G, w), BF) for _, w in CHUNKS],
+            *[V((NX - 1, ZL * G, w), BF) for _, w in CHUNKS],
+            V((ZL * G + 16, max(w for _, w in CHUNKS)), F32),
+            *[V((ZL, 48, w), BF) for _, w in CHUNKS],
+            V((ZL, 48, D), F32),
+            *[V((ZL - 1, 48, w), BF) for _, w in CHUNKS],
             V((48, D), F32),
             V((48, D), BF),
             V((NY - 1, 48, 256), BF),
-            V((48, 256), BF),
-            V((ZH - 1, 48, 256), BF),
+            V((ZH, 48, 128), BF),
+            V((ZH, 48, 128), F32),
+            V((ZH - 1, 48, 128), BF),
             dma((3,)), dma((3,)), dma((2,)), dma((2,)), dma((2,)), dma((3,)), dma((3,)),
             dma, dma, dma, dma, dma, dma,
             dma((NCH * (NX - 1),)), dma((NCH * (NX - 1),)),
             dma((NCH * (ZL - 1),)), dma((NCH * (ZL - 1),)),
-            dma((NY - 1,)), dma((NY - 1,)), dma((ZH - 1,)), dma((ZH - 1,)),
+            dma((NY,)), dma((NY - 1,)), dma((ZH - 1,)), dma((ZH - 1,)),
         ],
         compiler_params=pltpu.CompilerParams(
-            collective_id=0, has_side_effects=True, vmem_limit_bytes=56 * 2**20
+            collective_id=0, has_side_effects=True, vmem_limit_bytes=44 * 2**20
         ),
         name="siglip_backward",
-    )(image_features, head_weight, text_embeddings, log_scale, logit_bias)
+    )(
+        *(
+            pltpu.with_memory_space_constraint(a, pltpu.HBM)
+            for a in (image_features, head_weight, text_embeddings)
+        ),
+        log_scale,
+        logit_bias,
+    )
+    return text_grad, head_t.T
 
 
 def solution(mesh):

time: 76.1 us -> 68.2 us (0.90)
  the two profiles are of different devices: /device:TPU:64 before, /device:TPU:56 now
where the time goes in v2:
time: 68.2 us; the launch traced here: 68 us
  Pallas kernels  64.3 us (94%)
  between operations  1.93 us (3%)
  local copies, waits for them, and re-layouts  1.82 us (3%)
    pallas_call x1, Pallas kernels, shards(): pl.pallas_call(kernel, out_shape=(pltpu.VMEM((R, D), F32), pltpu.VMEM((G,...  64.3 us
    unnamed x2, local copies, waits for them, and re-layouts  1.82 us

profile of v2, /device:TPU:56, one launch (start us, length us, event | category | flops | bytes accessed | tf_op | source)
XLA Modules:
  0.0 68.0 jit_solution(11439020450579774564)
XLA Ops:
  1.9 64.3 %siglip_backward.1 = (f32[384,1152]{1,0:T(8,128)S(1)}, f32[36,48]{1,0:T(8,128)S(1)}) custom-call(bf16[384,1152]{1,0:T(8,128)(2,1)} %x_hbm.1, bf16[1152,1152]{1,0:T(8,128)(2,1)} %w_hbm.1, bf16[384,1152]{1,0:T(8,128)(2,1)} %t_hbm.1, f32[1]{0:T(128)S(6)} %copy.11.ls_ref, f32[1]{0:T(128)S(6)} %copy.12.lb_ref), custom_call_target="tpu_custom_call" | custom-call | tf_op jit(solution)/shard_map/siglip_backward/pallas_call | solution.py:369
  66.2 1.2 %copy.9 = f32[384,1152]{1,0:T(8,128)} copy(f32[384,1152]{1,0:T(8,128)S(1)} %get-tuple-element.6) | data formatting | bytes 3538944
  67.4 0.6 copy.10

commit v3 on v2

--- a/solution.py
+++ b/solution.py
@@ -16,8 +16,10 @@
 NCH = D // CH
 G = 36
 PIECE = 128
-CHUNKS = ((0, 512), (512, 384), (896, 256))
-WINDOWS = ((0, 1, 2), (3, 4, 5), (6, 7))
+CHUNKS = ((0, 384), (384, 384))
+WINDOWS = ((0, 1), (2, 3, 4))
+FIRST, WIDE = D - 384, 384
+LAST_WINDOWS = (5, 6, 7)
 
 
 def mm(a, b, dims):
@@ -33,11 +35,12 @@
     x_hbm, w_hbm, t_hbm, ls_ref, lb_ref,
     tg_ref, hg_ref,
     xb, wb, traw, tb, proj, ib, cb, c1b, c2b, dyo, dys, dyr, dtf, pf, dtb, hacc,
-    xs0, xs1, xs2, xr0, xr1, xr2, sc, zs0, zs1, zs2, zf, zr0, zr1, zr2, yf, ys, yr, hs, hf, hr,
+    xs0, xs1, xr0, xr1, sc, zs0, zs1, zf, zr0, zr1, yf, ys, yr, hs, hf, hr,
+    za, zaf, zar, xa, xaf, xar,
     lsem, x2s, x2r, fws, fwr, dts, dtr, pxs, pxr, pts, ptr, dyss, dyrs,
-    xss, xrs, zss, zrs, yss, yrs, hss, hrs,
+    zas, zars, xas, xars, xss, xrs, zss, zrs, yss, yrs, hss, hrs,
 ):
-    xs, xr, zs, zr = (xs0, xs1, xs2), (xr0, xr1, xr2), (zs0, zs1, zs2), (zr0, zr1, zr2)
+    xs, xr, zs, zr = (xs0, xs1), (xr0, xr1), (zs0, zs1), (zr0, zr1)
     blk = lax.axis_index("blk")
     nar = lax.axis_index("narrow")
     c = blk % 2
@@ -245,12 +248,30 @@
             xs[k].at[to], xr[k].at[d - 1], xss.at[i], xrs.at[i], dev(to, zl, c, y, zh)
         )
 
+    def zacopy(d):
+        to = (zl + d) % ZL
+        return rcopy(za.at[to], zar.at[d - 1], zas.at[d - 1], zars.at[d - 1], dev(x, to, c, y, zh))
+
+    def xacopy(d):
+        to = (x + d) % NX
+        return rcopy(xa.at[to], xar.at[d - 1], xas.at[d - 1], xars.at[d - 1], dev(to, zl, c, y, zh))
+
+    def late(ks):
+        hacc[:, ks] += mm(dtb[c, :, 2 * R : 3 * R], xb[2 * R : 3 * R, ks], NN)
+
+    late(slice(FIRST, D))
+    for z in range(ZL):
+        for xx in range(NX):
+            o = (xx * ZL + z) * G
+            zaf[z, xx * G : (xx + 1) * G, :] = hacc[o : o + G, FIRST:D]
+        za[z] = zaf[z].astype(BF)
+    for d in (2, 1, 3):
+        zacopy(d).start()
     for k, (o, w) in enumerate(CHUNKS):
         ks = slice(o, o + w)
-        h = hacc[:, ks] + mm(dtb[c, :, 2 * R : 3 * R], xb[2 * R : 3 * R, ks], NN)
-        hacc[:, ks] = h
+        late(ks)
         for xx in range(NX):
-            xs[k][xx] = h[xx * ZL * G : (xx + 1) * ZL * G, :].astype(BF)
+            xs[k][xx] = hacc[xx * ZL * G : (xx + 1) * ZL * G, ks].astype(BF)
         for d in (2, 1, 3):
             xcopy(k, d).start()
 
@@ -316,12 +337,35 @@
         for to in WINDOWS[k]:
             pl.when(y != to)(ycopy(to).start)
 
+    def after_za():
+        s = zaf[zl]
+        for d in range(1, ZL):
+            zacopy(d).wait_recv()
+            s = s + zar[d - 1].astype(F32)
+        sc[0 : NX * G, 0:WIDE] = s
+        for xx in range(NX):
+            p = sc[xx * G : xx * G + 48, 0:WIDE]
+            xaf[xx] = p
+            xa[xx] = p.astype(BF)
+        for d in (2, 1, 3):
+            xacopy(d).start()
+
+    def after_xa():
+        s = xaf[x]
+        for d in range(1, NX):
+            xacopy(d).wait_recv()
+            s = s + xar[d - 1].astype(F32)
+        yf[:, FIRST:D] = s
+        ys[:, FIRST:D] = s.astype(BF)
+
+    after_za()
     after_x(0)
     after_x(1)
     after_z(0)
-    after_x(2)
+    after_xa()
     after_z(1)
-    after_z(2)
+    for to in LAST_WINDOWS:
+        pl.when(y != to)(ycopy(to).start)
     s = yf[:, pl.ds(pl.multiple_of(y * 128, 128), 256)]
     for d in range(1, NY):
         rcopy(ys.at[:, 0:256], yr.at[d - 1], yss.at[0], yrs.at[d - 1], partner).wait_recv()
@@ -349,11 +393,15 @@
         for p, core, slot in ((0, 0, 0), (2, 1, 0), (1, 0, 1)):
             x2copy(p, core, slot).wait_send()
 
-    for k in range(NCH):
+    for k in range(len(CHUNKS)):
         for d in range(1, NX):
             xcopy(k, d).wait_send()
         for d in range(1, ZL):
             zcopy(k, d).wait_send()
+    for d in range(1, ZL):
+        zacopy(d).wait_send()
+    for d in range(1, NX):
+        xacopy(d).wait_send()
     for to in range(NY):
         pl.when(y != to)(ycopy(to).wait_send)
     for d in range(1, ZH):
@@ -390,7 +438,7 @@
             V((D // 2, D), F32),
             *[V((NX, ZL * G, w), BF) for _, w in CHUNKS],
             *[V((NX - 1, ZL * G, w), BF) for _, w in CHUNKS],
-            V((ZL * G + 16, max(w for _, w in CHUNKS)), F32),
+            V((ZL * G + 16, max(WIDE, *(w for _, w in CHUNKS))), F32),
             *[V((ZL, 48, w), BF) for _, w in CHUNKS],
             V((ZL, 48, D), F32),
             *[V((ZL - 1, 48, w), BF) for _, w in CHUNKS],
@@ -400,8 +448,15 @@
             V((ZH, 48, 128), BF),
             V((ZH, 48, 128), F32),
             V((ZH - 1, 48, 128), BF),
+            V((ZL, NX * G, WIDE), BF),
+            V((ZL, NX * G, WIDE), F32),
+            V((ZL - 1, NX * G, WIDE), BF),
+            V((NX, 48, WIDE), BF),
+            V((NX, 48, WIDE), F32),
+            V((NX - 1, 48, WIDE), BF),
             dma((3,)), dma((3,)), dma((2,)), dma((2,)), dma((2,)), dma((3,)), dma((3,)),
             dma, dma, dma, dma, dma, dma,
+            *[dma((n,)) for n in (ZL - 1, ZL - 1, NX - 1, NX - 1)],
             dma((NCH * (NX - 1),)), dma((NCH * (NX - 1),)),
             dma((NCH * (ZL - 1),)), dma((NCH * (ZL - 1),)),
             dma((NY,)), dma((NY - 1,)), dma((ZH - 1,)), dma((ZH - 1,)),

time: 68.2 us -> 65.5 us (0.960)
  Pallas kernels: 64.3 us -> 61.6 us
    pallas_call x1, Pallas kernels: 64.3 us -> 61.6 us  [shards(): pl.pallas_call(kernel, out_shape=(pltpu.VMEM((R, D), F32), pltpu.VMEM((G,...]
where the time goes in v3:
time: 65.5 us; the launch traced here: 65.3 us
  Pallas kernels  61.6 us (94%)
  between operations  1.93 us (3%)
  local copies, waits for them, and re-layouts  1.82 us (3%)
    pallas_call x1, Pallas kernels, shards(): pl.pallas_call(kernel, out_shape=(pltpu.VMEM((R, D), F32), pltpu.VMEM((G,...  61.6 us
    unnamed x2, local copies, waits for them, and re-layouts  1.82 us

profile of v3, /device:TPU:56, one launch (start us, length us, event | category | flops | bytes accessed | tf_op | source)
XLA Modules:
  0.0 65.3 jit_solution(4328506998118613338)
XLA Ops:
  1.9 61.6 %siglip_backward.1 = (f32[384,1152]{1,0:T(8,128)S(1)}, f32[36,48]{1,0:T(8,128)S(1)}) custom-call(bf16[384,1152]{1,0:T(8,128)(2,1)} %x_hbm.1, bf16[1152,1152]{1,0:T(8,128)(2,1)} %w_hbm.1, bf16[384,1152]{1,0:T(8,128)(2,1)} %t_hbm.1, f32[1]{0:T(128)S(6)} %copy.11.ls_ref, f32[1]{0:T(128)S(6)} %copy.12.lb_ref), custom_call_target="tpu_custom_call" | custom-call | tf_op jit(solution)/shard_map/siglip_backward/pallas_call | solution.py:417
  63.5 1.2 %copy.9 = f32[384,1152]{1,0:T(8,128)} copy(f32[384,1152]{1,0:T(8,128)S(1)} %get-tuple-element.6) | data formatting | bytes 3538944
  64.7 0.6 copy.10
